TPU v7x, 256 devices: a whole 4x4x8 slice. The times are simulated.
256 devices in a mesh: quad: 8 (over z_lo, core), dom: 32 (over x, y, z_hi).
Axes of the slice: x: 4, y: 4, z: 8 (z_hi: 2, z_lo: 4; z = z_hi * 4 + z_lo), core: 2. Of those that a mesh axis runs over, the one named last changes fastest.
Arguments:
- probes: float32 [2, 64, 256, 128], P(None, None, 'dom'), may hold values from -6 to 6
- mass_weights: float32 [256, 128], P('dom'), may hold values from 0.8 to 1.25
- blocks: float32 [2, 256, 128, 128], P(None, 'dom'), may hold values from -4 to 4
- couplings: float32 [2, 6, 256, 128], P(None, None, 'dom'), may hold values from -0.25 to 0.25
Outputs:
- moments: float32 [64, 4, 2, 256, 128], P('quad', None, None, 'dom')
- projected: float32 [2, 8, 64, 64], replicated
All inputs are finite; a program needn't handle non-finite values.
Results may differ from a plain program's by a relative error of at most 0.0001.
Values sent between devices are 32-bit elements; how exact they have to be, the bound alone decides.
A program may use at most 64 MiB of HBM per device.

v0:
```python
import math
import jax
import jax.numpy as jnp
from jax import lax
from jax.sharding import PartitionSpec as P

NQ = 16
ITERS = 4
MOM = 4
PRECISE = lax.Precision.HIGHEST
RADIUS = 2.0
OFFSETS = (-3, -2, -1, 1, 2, 3)


def with_halo(cells, sides, width):
    for axis, dim in sides:
        count = lax.axis_size(axis)
        ends = count - 1
        head = lax.slice_in_dim(cells, 0, width, axis=dim)
        tail = lax.slice_in_dim(cells, cells.shape[dim] - width, cells.shape[dim], axis=dim)
        cells = jnp.concatenate(
            [
                lax.ppermute(tail, axis, [(i, (i + 1) % count) for i in range(ends)]),
                cells,
                lax.ppermute(head, axis, [((i + 1) % count, i) for i in range(ends)]),
            ],
            axis=dim,
        )
    return cells


def shift_angles(shift_index, total_shifts):
    return 2.0 * math.pi / total_shifts * (shift_index.astype(jnp.float32) + 0.5)


def moment_weights(angles, moment_count, scale):
    orders = jnp.arange(1, moment_count + 1, dtype=jnp.float32)
    phases = orders[:, None] * angles[None, :]
    return (scale * jnp.cos(phases), scale * jnp.sin(phases))


def sweep(field, padded, blocks, couplings, zmass_re, zmass_im, inverse_re, inverse_im, source):
    rim_depth = max(OFFSETS)
    line_count = field.shape[3]
    field_re = field[0]
    field_im = field[1]
    image_re = jnp.einsum("spxj,xij->spxi", field_re, blocks[0], precision=PRECISE) - jnp.einsum(
        "spxj,xij->spxi", field_im, blocks[1], precision=PRECISE
    )
    image_im = jnp.einsum("spxj,xij->spxi", field_im, blocks[0], precision=PRECISE) + jnp.einsum(
        "spxj,xij->spxi", field_re, blocks[1], precision=PRECISE
    )
    for position, offset in enumerate(OFFSETS):
        neighbour = padded[:, :, :, rim_depth + offset : rim_depth + offset + line_count]
        coup_re = couplings[0, position]
        coup_im = couplings[1, position]
        image_re = image_re + coup_re * neighbour[0] - coup_im * neighbour[1]
        image_im = image_im + coup_re * neighbour[1] + coup_im * neighbour[0]
    resid_re = source[0] - (zmass_re * field_re - zmass_im * field_im) + image_re
    resid_im = source[1] - (zmass_re * field_im + zmass_im * field_re) + image_im
    return jnp.stack(
        [
            field_re + resid_re * inverse_re - resid_im * inverse_im,
            field_im + resid_re * inverse_im + resid_im * inverse_re,
        ]
    )


def moment_block(field_part, weight_re, weight_im):
    sum_re = jnp.einsum("ks,spxi->pkxi", weight_re, field_part[0], precision=PRECISE) - jnp.einsum(
        "ks,spxi->pkxi", weight_im, field_part[1], precision=PRECISE
    )
    sum_im = jnp.einsum("ks,spxi->pkxi", weight_re, field_part[1], precision=PRECISE) + jnp.einsum(
        "ks,spxi->pkxi", weight_im, field_part[0], precision=PRECISE
    )
    return jnp.stack([sum_re, sum_im], axis=2)


def project(gram_re, gram_im, angles, scale):
    proj_re, proj_im = moment_weights(angles, 2 * MOM, scale)
    mixed_re = jnp.einsum("ks,spq->kpq", proj_re, gram_re, precision=PRECISE) - jnp.einsum(
        "ks,spq->kpq", proj_im, gram_im, precision=PRECISE
    )
    mixed_im = jnp.einsum("ks,spq->kpq", proj_re, gram_im, precision=PRECISE) + jnp.einsum(
        "ks,spq->kpq", proj_im, gram_re, precision=PRECISE
    )
    return jnp.stack([mixed_re, mixed_im])


def on_device(probes, mass_weights, blocks, couplings):
    rim_depth = max(OFFSETS)
    shift_count = NQ // lax.axis_size("quad")
    probe_count = probes.shape[1]
    owned_probes = probe_count // lax.axis_size("quad")
    line_count = probes.shape[2]
    row_width = probes.shape[3]
    total_lines = line_count * lax.axis_size("dom")
    shift_index = lax.axis_index("quad") * shift_count + jnp.arange(shift_count, dtype=jnp.int32)
    angles = shift_angles(shift_index, NQ)
    zmass_re = (RADIUS * jnp.cos(angles))[:, None, None, None] * mass_weights[None, None]
    zmass_im = (RADIUS * jnp.sin(angles))[:, None, None, None] * mass_weights[None, None]
    diagonal = jnp.diagonal(blocks, axis1=2, axis2=3)
    denom_re = zmass_re - diagonal[0]
    denom_im = zmass_im - diagonal[1]
    modulus = denom_re * denom_re + denom_im * denom_im
    inverse_re = denom_re / modulus
    inverse_im = -denom_im / modulus
    source = mass_weights[None, None] * probes
    field = jnp.stack(
        [
            source[0] * inverse_re - source[1] * inverse_im,
            source[0] * inverse_im + source[1] * inverse_re,
        ]
    )
    for step in range(ITERS - 1):
        padded = with_halo(field, (("dom", 3),), rim_depth)
        field = sweep(
            field, padded, blocks, couplings, zmass_re, zmass_im, inverse_re, inverse_im, source
        )
    weight_re, weight_im = moment_weights(angles, MOM, RADIUS / NQ)
    field_rows = lax.slice_in_dim(field, 0, owned_probes * lax.axis_size("quad"), axis=2)
    moments = lax.psum_scatter(
        moment_block(field_rows, weight_re, weight_im), "quad", scatter_dimension=0, tiled=True
    )
    gram_re = jnp.einsum("pxi,sqxi->spq", probes[0], field[0], precision=PRECISE) + jnp.einsum(
        "pxi,sqxi->spq", probes[1], field[1], precision=PRECISE
    )
    gram_im = jnp.einsum("pxi,sqxi->spq", probes[0], field[1], precision=PRECISE) - jnp.einsum(
        "pxi,sqxi->spq", probes[1], field[0], precision=PRECISE
    )
    scale = RADIUS / (NQ * total_lines * row_width)
    projected = lax.psum(project(gram_re, gram_im, angles, scale), ("quad", "dom"))
    return (moments, projected)


def solution(mesh):
    return jax.shard_map(
        on_device,
        mesh=mesh,
        in_specs=(
            P(None, None, "dom", None),
            P("dom", None),
            P(None, "dom", None, None),
            P(None, None, "dom", None),
        ),
        out_specs=(P("quad", None, None, "dom", None), P()),
        check_vma=False,
    )
```

profile of v0, /device:TPU:2, one launch (start us, length us, event | category | flops | bytes accessed | tf_op | source)
XLA Modules:
  0.0 444.9 jit_solution(10704677841827037540)
XLA Ops:
  8.0 0.0 all-reduce.2.cloned.1.call-start
  8.1 0.0 copy-start.3
  8.1 13.3 %copy.50 = f32[2,8,128,128]{1,0,3,2:T(2,128)} copy(f32[2,8,128,128]{3,2,1,0:T(8,128)} %param.6) | data formatting | bytes 2097152 | tf_op args[2]
  21.3 6.7 %gather_fusion = f32[128,2,8]{2,1,0:T(2,128)S(1)} fusion(f32[2,8,128,128]{1,0,3,2:T(2,128)} %copy.50, s32[128]{0:T(128)S(1)} %or_bitcast_fusion), kind=kCustom, calls=%fused_computation | custom fusion | bytes 17408 | tf_op jit(solution)/shard_map/jit(diagonal)/gather | solution.py:102
  28.0 0.1 fusion.130
  28.2 0.1 copy.51
  28.3 0.1 sine_multiply_fusion
  28.4 0.1 copy.53
  28.5 0.1 copy.49
  28.6 0.1 fusion.78
  28.7 0.0 copy-start
  28.7 0.2 multiply_subtract_fusion.3
  28.8 0.1 pad_maximum_fusion.9
  28.9 11.7 %collective-permute-start.1 = (f32[2,2,64,3,128]{4,2,1,3,0:T(8,128)S(1)}, f32[2,2,64,3,128]{4,2,1,3,0:T(8,128)S(1)}, u32[]{:S(2)}, u32[]{:S(2)}) collective-permute-start(f32[2,2,64,3,128]{4,2,1,3,0:T(8,128)S(1)} %get-tuple-element.24), channel_id=1, source_target_pairs={{1,0},{2,1},{3,2},{4,3},{5,4},{6,5},{7,6},{8,7},{9,8},{10,9},{11,1... | collective-permute-start | bytes 1179656 | tf_op jit(solution)/shard_map/ppermute | solution.py:25
  40.6 1.9 collective-permute-start
  42.5 1.2 fusion.30
  43.9 1.2 fusion.28
  45.1 7.2 %collective-permute-done.1 = f32[2,2,64,3,128]{4,2,1,3,0:T(8,128)S(1)} collective-permute-done((f32[2,2,64,3,128]{4,2,1,3,0:T(8,128)S(1)}, f32[2,2,64,3,128]{4,2,1,3,0:T(8,128)S(1)}, u32[]{:S(2)}, u32[]{:S(2)}) %collective-permute-start.1) | collective-permute-done | bytes 393248 | tf_op jit(solution)/shard_map/ppermute | solution.py:25
  52.3 21.3 %collective-permute-done = f32[2,2,64,3,128]{4,2,1,3,0:T(8,128)S(1)} collective-permute-done((f32[2,2,64,3,128]{4,2,1,3,0:T(8,128)S(1)}, f32[2,2,64,3,128]{4,2,1,3,0:T(8,128)S(1)}, u32[]{:S(2)}, u32[]{:S(2)}) %collective-permute-start) | collective-permute-done | bytes 393248 | tf_op jit(solution)/shard_map/ppermute | solution.py:23
  73.6 0.4 pad_maximum_fusion.1
  74.0 1.9 subtract_add_fusion.2
  75.9 2.2 multiply_add_fusion.2
  78.1 0.1 pad_maximum_fusion.7
  78.2 8.9 %collective-permute-start.3 = (f32[2,2,64,3,128]{4,2,1,3,0:T(8,128)S(1)}, f32[2,2,64,3,128]{4,2,1,3,0:T(8,128)S(1)}, u32[]{:S(2)}, u32[]{:S(2)}) collective-permute-start(f32[2,2,64,3,128]{4,2,1,3,0:T(8,128)S(1)} %get-tuple-element.20), channel_id=1, source_target_pairs={{1,0},{2,1},{3,2},{4,3},{5,4},{6,5},{7,6},{8,7},{9,8},{10,9},{11,1... | collective-permute-start | bytes 1179656 | tf_op jit(solution)/shard_map/ppermute | solution.py:25
  87.1 1.9 collective-permute-start.2
  89.0 1.2 fusion.26
  90.3 1.2 fusion.24
  91.5 12.3 %collective-permute-done.3 = f32[2,2,64,3,128]{4,2,1,3,0:T(8,128)S(1)} collective-permute-done((f32[2,2,64,3,128]{4,2,1,3,0:T(8,128)S(1)}, f32[2,2,64,3,128]{4,2,1,3,0:T(8,128)S(1)}, u32[]{:S(2)}, u32[]{:S(2)}) %collective-permute-start.3) | collective-permute-done | bytes 393248 | tf_op jit(solution)/shard_map/ppermute | solution.py:25
  103.8 8.8 %collective-permute-done.2 = f32[2,2,64,3,128]{4,2,1,3,0:T(8,128)S(1)} collective-permute-done((f32[2,2,64,3,128]{4,2,1,3,0:T(8,128)S(1)}, f32[2,2,64,3,128]{4,2,1,3,0:T(8,128)S(1)}, u32[]{:S(2)}, u32[]{:S(2)}) %collective-permute-start.2) | collective-permute-done | bytes 393248 | tf_op jit(solution)/shard_map/ppermute | solution.py:23
  112.6 0.4 pad_maximum_fusion.2
  112.9 1.8 subtract_add_fusion.1
  114.8 2.1 multiply_add_fusion.1
  116.8 0.1 pad_maximum_fusion.5
  116.9 7.4 %collective-permute-start.5 = (f32[2,2,64,3,128]{4,2,1,3,0:T(8,128)S(1)}, f32[2,2,64,3,128]{4,2,1,3,0:T(8,128)S(1)}, u32[]{:S(2)}, u32[]{:S(2)}) collective-permute-start(f32[2,2,64,3,128]{4,2,1,3,0:T(8,128)S(1)} %get-tuple-element.16), channel_id=1, source_target_pairs={{1,0},{2,1},{3,2},{4,3},{5,4},{6,5},{7,6},{8,7},{9,8},{10,9},{11,1... | collective-permute-start | bytes 1179656 | tf_op jit(solution)/shard_map/ppermute | solution.py:25
  124.3 3.7 collective-permute-start.4
  128.1 1.2 fusion.22
  129.3 1.2 fusion.20
  130.5 1.3 collective-permute-done.5
  131.8 22.8 %collective-permute-done.4 = f32[2,2,64,3,128]{4,2,1,3,0:T(8,128)S(1)} collective-permute-done((f32[2,2,64,3,128]{4,2,1,3,0:T(8,128)S(1)}, f32[2,2,64,3,128]{4,2,1,3,0:T(8,128)S(1)}, u32[]{:S(2)}, u32[]{:S(2)}) %collective-permute-start.4) | collective-permute-done | bytes 393248 | tf_op jit(solution)/shard_map/ppermute | solution.py:23
  154.6 0.3 pad_maximum_fusion.3
  154.8 1.9 subtract_add_fusion
  156.8 2.1 multiply_subtract_fusion
  158.8 2.2 fusion.36
  161.0 2.2 fusion.40
  163.2 0.6 convolution_bitcast_fusion
  163.8 0.6 convolution_bitcast_fusion.2
  164.4 2.5 fusion
  166.9 2.3 fusion.1
  169.2 0.6 fusion.13
  169.8 0.1 copy.64
  169.9 0.6 fusion.11
  170.5 0.1 copy.63
  170.6 0.5 fusion.89
  171.1 0.5 fusion.91
  171.7 0.5 fusion.9
  172.2 0.5 fusion.8
  172.7 0.8 pad_maximum_fusion.4
  173.6 0.0 all-reduce.2.cloned.1.call-update
  173.6 0.0 reduce-scatter.2.cloned.1.call-start
  173.7 0.5 pad_maximum_fusion
  174.2 1.5 copy.60
  175.7 0.0 reduce-scatter.2.cloned.1.call-update
  175.8 259.7 %all-reduce.2.cloned.1.call-done = f32[2,8,64,64]{3,1,2,0:T(8,128)} async-done(((f32[2,8,64,64]{3,1,2,0:T(8,128)}), f32[2,8,64,64]{3,1,2,0:T(8,128)}) %all-reduce.2.cloned.1.call-update) | async-done | bytes 262160 | tf_op jit(solution)/shard_map/psum | solution.py:132
  435.5 1.9 copy.67
  (16 shorter events, 0.2 us)
Async XLA Ops:
  8.0 427.5 %all-reduce.2.cloned.1.call-start = ((), (), s32[]{:S(2)}) async-start(), calls=%async_computation.2 | async-start | bytes 1048576 | tf_op jit(solution)/shard_map/psum | solution.py:132
  8.1 20.3 %copy-start.1 = (f32[2,64,8,128]{3,2,1,0:T(8,128)S(1)}, f32[2,64,8,128]{3,2,1,0:T(8,128)}, u32[]{:S(2)}) copy-start(f32[2,64,8,128]{3,2,1,0:T(8,128)} %param.4) | copy-start | bytes 1572868
  8.1 20.3 %copy-start.3 = (f32[8,128]{1,0:T(8,128)S(1)}, f32[8,128]{1,0:T(8,128)}, u32[]{:S(2)}) copy-start(f32[8,128]{1,0:T(8,128)} %param.5) | copy-start | bytes 12292
  28.7 13.9 %copy-start = (f32[2,8,128,128]{3,2,1,0:T(8,128)S(1)}, f32[2,8,128,128]{3,2,1,0:T(8,128)}, u32[]{:S(2)}) copy-start(f32[2,8,128,128]{3,2,1,0:T(8,128)} %param.6) | copy-start | bytes 3145732
  28.9 14.9 %copy-start.2 = (f32[2,6,8,128]{3,2,1,0:T(8,128)S(1)}, f32[2,6,8,128]{3,2,1,0:T(8,128)}, u32[]{:S(2)}) copy-start(f32[2,6,8,128]{3,2,1,0:T(8,128)} %param.7) | copy-start | bytes 147460
  28.9 23.3 %collective-permute-start.1 = (f32[2,2,64,3,128]{4,2,1,3,0:T(8,128)S(1)}, f32[2,2,64,3,128]{4,2,1,3,0:T(8,128)S(1)}, u32[]{:S(2)}, u32[]{:S(2)}) collective-permute-start(f32[2,2,64,3,128]{4,2,1,3,0:T(8,128)S(1)} %get-tuple-element.24), channel_id=1, source_target_pairs={{1,0},{2,1},{3,2},{4,3},{5,4},{6,5},{7,6},{8,7},{9,8},{10,9},{11,1... | collective-permute-start | bytes 1179656 | tf_op jit(solution)/shard_map/ppermute | solution.py:25
  40.6 33.0 %collective-permute-start = (f32[2,2,64,3,128]{4,2,1,3,0:T(8,128)S(1)}, f32[2,2,64,3,128]{4,2,1,3,0:T(8,128)S(1)}, u32[]{:S(2)}, u32[]{:S(2)}) collective-permute-start(f32[2,2,64,3,128]{4,2,1,3,0:T(8,128)S(1)} %get-tuple-element.25), channel_id=1, source_target_pairs={{0,1},{1,2},{2,3},{3,4},{4,5},{5,6},{6,7},{7,8},{8,9},{9,10},{10,1... | collective-permute-start | bytes 1179656 | tf_op jit(solution)/shard_map/ppermute | solution.py:23
  78.2 25.6 %collective-permute-start.3 = (f32[2,2,64,3,128]{4,2,1,3,0:T(8,128)S(1)}, f32[2,2,64,3,128]{4,2,1,3,0:T(8,128)S(1)}, u32[]{:S(2)}, u32[]{:S(2)}) collective-permute-start(f32[2,2,64,3,128]{4,2,1,3,0:T(8,128)S(1)} %get-tuple-element.20), channel_id=1, source_target_pairs={{1,0},{2,1},{3,2},{4,3},{5,4},{6,5},{7,6},{8,7},{9,8},{10,9},{11,1... | collective-permute-start | bytes 1179656 | tf_op jit(solution)/shard_map/ppermute | solution.py:25
  87.1 25.5 %collective-permute-start.2 = (f32[2,2,64,3,128]{4,2,1,3,0:T(8,128)S(1)}, f32[2,2,64,3,128]{4,2,1,3,0:T(8,128)S(1)}, u32[]{:S(2)}, u32[]{:S(2)}) collective-permute-start(f32[2,2,64,3,128]{4,2,1,3,0:T(8,128)S(1)} %get-tuple-element.21), channel_id=1, source_target_pairs={{0,1},{1,2},{2,3},{3,4},{4,5},{5,6},{6,7},{7,8},{8,9},{9,10},{10,1... | collective-permute-start | bytes 1179656 | tf_op jit(solution)/shard_map/ppermute | solution.py:23
  116.9 14.9 %collective-permute-start.5 = (f32[2,2,64,3,128]{4,2,1,3,0:T(8,128)S(1)}, f32[2,2,64,3,128]{4,2,1,3,0:T(8,128)S(1)}, u32[]{:S(2)}, u32[]{:S(2)}) collective-permute-start(f32[2,2,64,3,128]{4,2,1,3,0:T(8,128)S(1)} %get-tuple-element.16), channel_id=1, source_target_pairs={{1,0},{2,1},{3,2},{4,3},{5,4},{6,5},{7,6},{8,7},{9,8},{10,9},{11,1... | collective-permute-start | bytes 1179656 | tf_op jit(solution)/shard_map/ppermute | solution.py:25
  124.3 30.2 %collective-permute-start.4 = (f32[2,2,64,3,128]{4,2,1,3,0:T(8,128)S(1)}, f32[2,2,64,3,128]{4,2,1,3,0:T(8,128)S(1)}, u32[]{:S(2)}, u32[]{:S(2)}) collective-permute-start(f32[2,2,64,3,128]{4,2,1,3,0:T(8,128)S(1)} %get-tuple-element.17), channel_id=1, source_target_pairs={{0,1},{1,2},{2,3},{3,4},{4,5},{5,6},{6,7},{7,8},{8,9},{9,10},{10,1... | collective-permute-start | bytes 1179656 | tf_op jit(solution)/shard_map/ppermute | solution.py:23
  173.6 263.8 %reduce-scatter.2.cloned.1.call-start = ((), (), s32[]{:S(2)}) async-start(), calls=%async_computation.1 | async-start | bytes 2359296 | tf_op jit(solution)/shard_map/reduce_scatter | solution.py:122
Sparse Core Ops, SparseCore 0:
  173.7 261.7 all-reduce.1
Sparse Core Ops, SparseCore 1:
  177.2 49.0 reduce-scatter.1
where the time goes:
time: 446 us; the launch traced here: 445 us
  waiting for transfers between devices  333 us (75%)
  starting transfers between devices  35.6 us (8%)
  matrix products  32.9 us (7%)
  local copies, waits for them, and re-layouts  24 us (5%)
  between operations  15.9 us (4%)
    psum x1, waiting for transfers between devices, on_device(): lax.psum(project(gram_re, gram_im, angles, scale), ('quad', 'dom'))  260 us
    ppermute x3, waiting for transfers between devices, with_halo(): lax.ppermute(tail, axis, [(i, (i + 1) % count) for i in range(ends)])  52.9 us
    ppermute x3, starting transfers between devices, with_halo(): lax.ppermute(head, axis, [((i + 1) % count, i) for i in range(ends)])  28 us
    ppermute x3, waiting for transfers between devices, with_halo(): lax.ppermute(head, axis, [((i + 1) % count, i) for i in range(ends)])  20.8 us
    unnamed x10, local copies, waits for them, and re-layouts  15.2 us
  transfers between devices with their start and end apart: 8, of which 7 were waited for; matrix products, arithmetic and copies ran while one was open for 3% of the time, Pallas kernels for 0%

commit v1 on v0

--- a/solution.py
+++ b/solution.py
@@ -129,7 +129,7 @@
         "pxi,sqxi->spq", probes[1], field[0], precision=PRECISE
     )
     scale = RADIUS / (NQ * total_lines * row_width)
-    projected = lax.psum(project(gram_re, gram_im, angles, scale), ("quad", "dom"))
+    projected = lax.psum(lax.psum(project(gram_re, gram_im, angles, scale), "quad"), "dom")
     return (moments, projected)
 
 

time: 446 us -> 728 us (1.63)
  waiting for transfers between devices: 333 us -> 617 us
    psum x1 -> x2, waiting for transfers between devices: 260 us -> 497 us  [the longest x1 419 us: on_device(): lax.psum(lax.psum(project(gram_re, gram_im, angles, scale), 'quad'), 'dom')]
    reduce_scatter x1, waiting for transfers between devices: 0.01 us -> 46.7 us  [on_device(): lax.psum_scatter(moment_block(field_rows, weight_re, weight_im), 'quad',...]
  transfers between devices with their start and end apart: 8 -> 9, of which waited for: 7 -> 9; matrix products, arithmetic and copies ran while one was open for 3% -> 2% of each run, Pallas kernels for 0% -> 0%
where the time goes in v1:
time: 728 us; the launch traced here: 727 us
  waiting for transfers between devices  617 us (85%)
  starting transfers between devices  35.8 us (5%)
  matrix products  32.7 us (4%)
  local copies, waits for them, and re-layouts  24 us (3%)
  between operations  14.2 us (2%)
    psum x1, waiting for transfers between devices, on_device(): lax.psum(lax.psum(project(gram_re, gram_im, angles, scale), 'quad'), 'dom')  419 us
    psum x1, waiting for transfers between devices, on_device(): lax.psum(project(gram_re, gram_im, angles, scale), 'quad')  77.8 us
    ppermute x3, waiting for transfers between devices, with_halo(): lax.ppermute(tail, axis, [(i, (i + 1) % count) for i in range(ends)])  52.1 us
    reduce_scatter x1, waiting for transfers between devices, on_device(): lax.psum_scatter(moment_block(field_rows, weight_re, weight_im), 'quad',...  46.7 us
    ppermute x3, starting transfers between devices, with_halo(): lax.ppermute(head, axis, [((i + 1) % count, i) for i in range(ends)])  28 us
    ppermute x3, waiting for transfers between devices, with_halo(): lax.ppermute(head, axis, [((i + 1) % count, i) for i in range(ends)])  21.4 us
    unnamed x10, local copies, waits for them, and re-layouts  15.2 us
  transfers between devices with their start and end apart: 9, of which 9 were waited for; matrix products, arithmetic and copies ran while one was open for 2% of the time, Pallas kernels for 0%

profile of v1, /device:TPU:2, one launch (start us, length us, event | category | flops | bytes accessed | tf_op | source)
XLA Modules:
  0.0 726.6 jit_solution(16513765652101253332)
XLA Ops:
  7.2 0.0 all-reduce.3.cloned.1.call-start
  7.2 13.3 %copy.50 = f32[2,8,128,128]{1,0,3,2:T(2,128)} copy(f32[2,8,128,128]{3,2,1,0:T(8,128)} %param.6) | data formatting | bytes 2097152 | tf_op args[2]
  20.5 6.7 gather_fusion
  27.2 0.1 fusion.130
  27.4 0.1 copy.51
  27.4 0.1 sine_multiply_fusion
  27.6 0.1 copy.53
  27.7 0.1 copy.49
  27.7 0.1 fusion.78
  27.8 0.1 multiply_subtract_fusion.3
  28.0 0.1 pad_maximum_fusion.9
  28.1 11.7 %collective-permute-start.1 = (f32[2,2,64,3,128]{4,2,1,3,0:T(8,128)S(1)}, f32[2,2,64,3,128]{4,2,1,3,0:T(8,128)S(1)}, u32[]{:S(2)}, u32[]{:S(2)}) collective-permute-start(f32[2,2,64,3,128]{4,2,1,3,0:T(8,128)S(1)} %get-tuple-element.24), channel_id=1, source_target_pairs={{1,0},{2,1},{3,2},{4,3},{5,4},{6,5},{7,6},{8,7},{9,8},{10,9},{11,1... | collective-permute-start | bytes 1179656 | tf_op jit(solution)/shard_map/ppermute | solution.py:25
  39.7 1.9 collective-permute-start
  41.7 1.2 fusion.30
  43.0 1.2 fusion.28
  44.2 7.2 collective-permute-done.1
  51.4 21.3 %collective-permute-done = f32[2,2,64,3,128]{4,2,1,3,0:T(8,128)S(1)} collective-permute-done((f32[2,2,64,3,128]{4,2,1,3,0:T(8,128)S(1)}, f32[2,2,64,3,128]{4,2,1,3,0:T(8,128)S(1)}, u32[]{:S(2)}, u32[]{:S(2)}) %collective-permute-start) | collective-permute-done | bytes 393248 | tf_op jit(solution)/shard_map/ppermute | solution.py:23
  72.7 0.4 pad_maximum_fusion.1
  73.1 1.9 subtract_add_fusion.2
  75.0 2.2 multiply_add_fusion.2
  77.2 0.1 pad_maximum_fusion.7
  77.3 8.9 %collective-permute-start.3 = (f32[2,2,64,3,128]{4,2,1,3,0:T(8,128)S(1)}, f32[2,2,64,3,128]{4,2,1,3,0:T(8,128)S(1)}, u32[]{:S(2)}, u32[]{:S(2)}) collective-permute-start(f32[2,2,64,3,128]{4,2,1,3,0:T(8,128)S(1)} %get-tuple-element.20), channel_id=1, source_target_pairs={{1,0},{2,1},{3,2},{4,3},{5,4},{6,5},{7,6},{8,7},{9,8},{10,9},{11,1... | collective-permute-start | bytes 1179656 | tf_op jit(solution)/shard_map/ppermute | solution.py:25
  86.2 1.9 collective-permute-start.2
  88.2 1.2 fusion.26
  89.4 1.2 fusion.24
  90.6 12.9 %collective-permute-done.3 = f32[2,2,64,3,128]{4,2,1,3,0:T(8,128)S(1)} collective-permute-done((f32[2,2,64,3,128]{4,2,1,3,0:T(8,128)S(1)}, f32[2,2,64,3,128]{4,2,1,3,0:T(8,128)S(1)}, u32[]{:S(2)}, u32[]{:S(2)}) %collective-permute-start.3) | collective-permute-done | bytes 393248 | tf_op jit(solution)/shard_map/ppermute | solution.py:25
  103.5 8.1 %collective-permute-done.2 = f32[2,2,64,3,128]{4,2,1,3,0:T(8,128)S(1)} collective-permute-done((f32[2,2,64,3,128]{4,2,1,3,0:T(8,128)S(1)}, f32[2,2,64,3,128]{4,2,1,3,0:T(8,128)S(1)}, u32[]{:S(2)}, u32[]{:S(2)}) %collective-permute-start.2) | collective-permute-done | bytes 393248 | tf_op jit(solution)/shard_map/ppermute | solution.py:23
  111.6 0.4 pad_maximum_fusion.2
  112.0 1.8 subtract_add_fusion.1
  113.8 2.0 multiply_add_fusion.1
  115.8 0.1 pad_maximum_fusion.5
  115.9 7.5 %collective-permute-start.5 = (f32[2,2,64,3,128]{4,2,1,3,0:T(8,128)S(1)}, f32[2,2,64,3,128]{4,2,1,3,0:T(8,128)S(1)}, u32[]{:S(2)}, u32[]{:S(2)}) collective-permute-start(f32[2,2,64,3,128]{4,2,1,3,0:T(8,128)S(1)} %get-tuple-element.16), channel_id=1, source_target_pairs={{1,0},{2,1},{3,2},{4,3},{5,4},{6,5},{7,6},{8,7},{9,8},{10,9},{11,1... | collective-permute-start | bytes 1179656 | tf_op jit(solution)/shard_map/ppermute | solution.py:25
  123.3 3.8 collective-permute-start.4
  127.1 1.2 fusion.22
  128.3 1.2 fusion.20
  129.6 1.3 collective-permute-done.5
  130.9 22.7 %collective-permute-done.4 = f32[2,2,64,3,128]{4,2,1,3,0:T(8,128)S(1)} collective-permute-done((f32[2,2,64,3,128]{4,2,1,3,0:T(8,128)S(1)}, f32[2,2,64,3,128]{4,2,1,3,0:T(8,128)S(1)}, u32[]{:S(2)}, u32[]{:S(2)}) %collective-permute-start.4) | collective-permute-done | bytes 393248 | tf_op jit(solution)/shard_map/ppermute | solution.py:23
  153.6 0.4 pad_maximum_fusion.3
  153.9 1.8 subtract_add_fusion
  155.7 2.0 multiply_subtract_fusion
  157.8 0.6 convolution_bitcast_fusion
  158.3 0.6 convolution_bitcast_fusion.2
  158.9 2.2 fusion.36
  161.1 2.4 fusion
  163.5 0.6 fusion.13
  164.0 0.1 copy.64
  164.1 0.6 fusion.11
  164.7 0.1 copy.63
  164.8 0.5 fusion.89
  165.4 0.5 fusion.91
  165.9 0.8 fusion.9
  166.7 0.5 fusion.8
  167.2 0.8 pad_maximum_fusion.4
  168.1 0.0 all-reduce.5.cloned.1.call-start
  168.2 2.2 fusion.40
  170.4 77.8 %all-reduce.3.cloned.1.call-done = f32[2,8,64,64]{3,1,2,0:T(8,128)} async-done(((f32[2,8,64,64]{3,1,2,0:T(8,128)}), f32[2,8,64,64]{3,1,2,0:T(8,128)}) %all-reduce.3.cloned.1.call-update) | async-done | bytes 262160 | tf_op jit(solution)/shard_map/psum | solution.py:132
  248.1 0.0 all-reduce.5.cloned.1.call-update
  248.2 0.0 reduce-scatter.2.cloned.1.call-start
  248.2 2.2 fusion.1
  250.5 0.5 pad_maximum_fusion
  251.0 1.5 copy.60
  252.6 418.9 %all-reduce.5.cloned.1.call-done = f32[2,8,64,64]{3,1,2,0:T(8,128)} async-done(((f32[2,8,64,64]{3,1,2,0:T(8,128)}), f32[2,8,64,64]{3,1,2,0:T(8,128)}) %all-reduce.5.cloned.1.call-update) | async-done | bytes 262160 | tf_op jit(solution)/shard_map/psum | solution.py:132
  671.4 1.9 copy.67
  673.4 46.7 %reduce-scatter.2.cloned.1.call-done = f32[8,4,2,8,128]{4,3,2,1,0:T(8,128)} async-done(((f32[64,4,2,8,128]{4,3,2,1,0:T(8,128)}), f32[8,4,2,8,128]{4,3,2,1,0:T(8,128)}) %reduce-scatter.2.cloned.1.call-update) | async-done | bytes 262160 | tf_op jit(solution)/shard_map/reduce_scatter | solution.py:122
  (19 shorter events, 0.3 us)
Async XLA Ops:
  7.2 241.0 %all-reduce.3.cloned.1.call-start = ((), (), s32[]{:S(2)}) async-start(), calls=%async_computation.2 | async-start | bytes 1048576 | tf_op jit(solution)/shard_map/psum | solution.py:132
  7.2 20.3 %copy-start.1 = (f32[2,64,8,128]{3,2,1,0:T(8,128)S(1)}, f32[2,64,8,128]{3,2,1,0:T(8,128)}, u32[]{:S(2)}) copy-start(f32[2,64,8,128]{3,2,1,0:T(8,128)} %param.4) | copy-start | bytes 1572868
  7.2 20.3 %copy-start.3 = (f32[8,128]{1,0:T(8,128)S(1)}, f32[8,128]{1,0:T(8,128)}, u32[]{:S(2)}) copy-start(f32[8,128]{1,0:T(8,128)} %param.5) | copy-start | bytes 12292
  27.8 13.8 %copy-start = (f32[2,8,128,128]{3,2,1,0:T(8,128)S(1)}, f32[2,8,128,128]{3,2,1,0:T(8,128)}, u32[]{:S(2)}) copy-start(f32[2,8,128,128]{3,2,1,0:T(8,128)} %param.6) | copy-start | bytes 3145732
  28.1 14.9 %copy-start.2 = (f32[2,6,8,128]{3,2,1,0:T(8,128)S(1)}, f32[2,6,8,128]{3,2,1,0:T(8,128)}, u32[]{:S(2)}) copy-start(f32[2,6,8,128]{3,2,1,0:T(8,128)} %param.7) | copy-start | bytes 147460
  28.1 23.3 %collective-permute-start.1 = (f32[2,2,64,3,128]{4,2,1,3,0:T(8,128)S(1)}, f32[2,2,64,3,128]{4,2,1,3,0:T(8,128)S(1)}, u32[]{:S(2)}, u32[]{:S(2)}) collective-permute-start(f32[2,2,64,3,128]{4,2,1,3,0:T(8,128)S(1)} %get-tuple-element.24), channel_id=1, source_target_pairs={{1,0},{2,1},{3,2},{4,3},{5,4},{6,5},{7,6},{8,7},{9,8},{10,9},{11,1... | collective-permute-start | bytes 1179656 | tf_op jit(solution)/shard_map/ppermute | solution.py:25
  39.7 33.0 %collective-permute-start = (f32[2,2,64,3,128]{4,2,1,3,0:T(8,128)S(1)}, f32[2,2,64,3,128]{4,2,1,3,0:T(8,128)S(1)}, u32[]{:S(2)}, u32[]{:S(2)}) collective-permute-start(f32[2,2,64,3,128]{4,2,1,3,0:T(8,128)S(1)} %get-tuple-element.25), channel_id=1, source_target_pairs={{0,1},{1,2},{2,3},{3,4},{4,5},{5,6},{6,7},{7,8},{8,9},{9,10},{10,1... | collective-permute-start | bytes 1179656 | tf_op jit(solution)/shard_map/ppermute | solution.py:23
  77.3 26.2 %collective-permute-start.3 = (f32[2,2,64,3,128]{4,2,1,3,0:T(8,128)S(1)}, f32[2,2,64,3,128]{4,2,1,3,0:T(8,128)S(1)}, u32[]{:S(2)}, u32[]{:S(2)}) collective-permute-start(f32[2,2,64,3,128]{4,2,1,3,0:T(8,128)S(1)} %get-tuple-element.20), channel_id=1, source_target_pairs={{1,0},{2,1},{3,2},{4,3},{5,4},{6,5},{7,6},{8,7},{9,8},{10,9},{11,1... | collective-permute-start | bytes 1179656 | tf_op jit(solution)/shard_map/ppermute | solution.py:25
  86.2 25.4 %collective-permute-start.2 = (f32[2,2,64,3,128]{4,2,1,3,0:T(8,128)S(1)}, f32[2,2,64,3,128]{4,2,1,3,0:T(8,128)S(1)}, u32[]{:S(2)}, u32[]{:S(2)}) collective-permute-start(f32[2,2,64,3,128]{4,2,1,3,0:T(8,128)S(1)} %get-tuple-element.21), channel_id=1, source_target_pairs={{0,1},{1,2},{2,3},{3,4},{4,5},{5,6},{6,7},{7,8},{8,9},{9,10},{10,1... | collective-permute-start | bytes 1179656 | tf_op jit(solution)/shard_map/ppermute | solution.py:23
  115.9 15.0 %collective-permute-start.5 = (f32[2,2,64,3,128]{4,2,1,3,0:T(8,128)S(1)}, f32[2,2,64,3,128]{4,2,1,3,0:T(8,128)S(1)}, u32[]{:S(2)}, u32[]{:S(2)}) collective-permute-start(f32[2,2,64,3,128]{4,2,1,3,0:T(8,128)S(1)} %get-tuple-element.16), channel_id=1, source_target_pairs={{1,0},{2,1},{3,2},{4,3},{5,4},{6,5},{7,6},{8,7},{9,8},{10,9},{11,1... | collective-permute-start | bytes 1179656 | tf_op jit(solution)/shard_map/ppermute | solution.py:25
  123.3 30.2 %collective-permute-start.4 = (f32[2,2,64,3,128]{4,2,1,3,0:T(8,128)S(1)}, f32[2,2,64,3,128]{4,2,1,3,0:T(8,128)S(1)}, u32[]{:S(2)}, u32[]{:S(2)}) collective-permute-start(f32[2,2,64,3,128]{4,2,1,3,0:T(8,128)S(1)} %get-tuple-element.17), channel_id=1, source_target_pairs={{0,1},{1,2},{2,3},{3,4},{4,5},{5,6},{6,7},{7,8},{8,9},{9,10},{10,1... | collective-permute-start | bytes 1179656 | tf_op jit(solution)/shard_map/ppermute | solution.py:23
  168.1 503.3 %all-reduce.5.cloned.1.call-start = ((), (), s32[]{:S(2)}) async-start(), calls=%async_computation.3 | async-start | bytes 1048576 | tf_op jit(solution)/shard_map/psum | solution.py:132
  248.2 471.9 %reduce-scatter.2.cloned.1.call-start = ((), (), s32[]{:S(2)}) async-start(), calls=%async_computation.1 | async-start | bytes 2359296 | tf_op jit(solution)/shard_map/reduce_scatter | solution.py:122
Sparse Core Ops, SparseCore 0:
  168.2 79.8 all-reduce.2
  250.9 420.4 all-reduce.4
  674.5 45.4 reduce-scatter.1
